TPU v7x, 32 devices: a whole 2x2x4 slice. The times are simulated.
32 devices in a mesh: wide: 16 (over z, y, x), narrow: 2 (over core).
Axes of the slice: x: 2, y: 2, z: 4, core: 2. Of those that a mesh axis runs over, the one named last changes fastest.
Arguments:
- tracers: float32 [13, 16, 64, 256], P(None, None, 'wide', 'narrow'), may hold values from -6 to 6
- courant_x: float32 [16, 64, 256], P(None, 'wide', 'narrow'), may hold values from -0.24 to 0.24
- courant_y: float32 [16, 64, 256], P(None, 'wide', 'narrow'), may hold values from -0.24 to 0.24
- physics_ref: float32 [13, 16], replicated, may hold values from -6 to 6
- class_coeffs: float32 [2, 3, 13], replicated, may hold values from 0.1 to 2
- span_target: int32 [64, 256], P('wide', 'narrow'), may hold values from 0 to 8191, as said below
- cloud_class: int32 [64, 256], P('wide', 'narrow'), may hold values from 0 to 2, as said below
Outputs:
- state_out: float32 [13, 16, 64, 256], P(None, None, 'wide', 'narrow')
- span_diag: float32 [64, 256], P('wide', 'narrow')
Inputs may be any that keep to these rules, and one draw needn't show every extreme that they name: `span_target`: within each block of 128 grid columns held by one index of narrow, the values are a permutation of 0 .. 8191; v names slot v % 512 of span v // 512, and a device's cell of local index r * 128 + c has grid position (row block start + r, column block start + c), a slot likewise in span order. Each device sends exactly 8 cells to every other span of its column block; its other cells go to its own span. `cloud_class`: A cell's class is that of its slot: slots 0 .. 63 of every span are class 2, the next 128 slots class 1, the rest class 0.
All inputs are finite; a program needn't handle non-finite values.
Results may differ from a plain program's by a relative error of at most 0.0001.
Values sent between devices are 32-bit elements; how exact they have to be, the bound alone decides.
No kernel may reach another device: no remote copies, remote signals or barrier semaphores. Data moves between devices by JAX's collectives and lax.ppermute only.
A program may use at most 64 MiB of HBM per device.

v0:
```python
import functools
import math

import jax
import jax.numpy as jnp
from jax import lax
from jax.experimental import pallas as pl
from jax.experimental.pallas import tpu as pltpu
from jax.sharding import PartitionSpec as P

VMEM = pl.BlockSpec(memory_space=pltpu.VMEM)
HBM = pl.BlockSpec(memory_space=pltpu.HBM)
SMEM = pl.BlockSpec(memory_space=pltpu.SMEM)
F32 = jnp.float32
PARAMS = pltpu.CompilerParams(vmem_limit_bytes=12 * 1024 * 1024)


def sub_roll(value, shift):
    shift = shift % value.shape[0]
    return value if shift == 0 else pltpu.roll(value, shift, 0)


def lane_roll(value, shift):
    shift = shift % value.shape[1]
    return value if shift == 0 else pltpu.roll(value, shift, 1)


def iotas(shape):
    return lax.broadcasted_iota(jnp.int32, shape, 0), lax.broadcasted_iota(jnp.int32, shape, 1)


def one_row(vectors, row, step):
    rows = vectors[0].shape[0] // 2
    local = iotas(vectors[0].shape)[0] % rows
    packed = []
    for start in range(0, len(vectors), rows):
        total = vectors[start]
        for t in range(1, rows):
            total = jnp.where(
                local == row + step * t, sub_roll(vectors[start + t], step * t), total
            )
        packed.append(total)
    return packed


def pack_north_kernel(levels, tracers_in, cx_in, cy_in, tracers, cx, cy, north, semaphores):
    copies = [
        pltpu.make_async_copy(source, into, semaphores.at[i])
        for i, (source, into) in enumerate(((tracers_in, tracers), (cx_in, cx), (cy_in, cy)))
    ]
    for copy in copies:
        copy.start()
    for copy in copies:
        copy.wait()
    pairs = levels // 2
    half = pairs // 2
    tile = tracers.shape[1:]
    rows = tile[0] // 2
    upper = iotas(tile)[0] % rows >= rows // 2
    fields = tracers.shape[0] // pairs
    for f in range(fields):
        for k in range(half):
            one, two = tracers[f * pairs + 2 * k], tracers[f * pairs + 2 * k + 1]
            north[f * half + k] = jnp.where(upper, one, sub_roll(two, 2))
    base = fields * half
    for k in range(half):
        north[base + k] = jnp.where(upper, cy[2 * k], sub_roll(cy[2 * k + 1], 2))
    for k, value in enumerate(one_row([cx[k] for k in range(pairs)], rows - 1, -1)):
        north[base + half + k] = value


def pack_edges_kernel(levels, tracers, cx, cy, edge, corner, south_rows):
    pairs = levels // 2
    half = pairs // 2
    fields = tracers.shape[0] // pairs
    tile = tracers.shape[1:]
    rows = tile[0] // 2
    lanes = tile[1]
    group = lanes // levels
    sub, lane = iotas(tile)
    upper = sub % rows >= rows // 2
    odd_sub = sub % 2 == 1
    corners = [jnp.zeros(tile, F32)]

    def pack_edge(vectors, slot):
        total = lane_roll(vectors[0], 2)
        for k in range(1, pairs):
            total = jnp.where(
                lane // (2 * group) == k, lane_roll(vectors[k], 2 + 2 * group * k), total
            )
        total = jnp.where(
            lane % (2 * group) < group, total, sub_roll(lane_roll(total, group), rows)
        )
        edge[slot] = jnp.where(lane % group < group // 2, total, lane_roll(total, group // 2))
        for k in range(half):
            one, two = vectors[2 * k], vectors[2 * k + 1]
            place = slot * half + k
            north = jnp.where(upper, one, sub_roll(two, 2))
            south = jnp.where(upper, sub_roll(two, -2), one)
            if slot < fields:
                south_rows[place] = south
            value = lane_roll(jnp.where(odd_sub, north, south), 2 * place + 1)
            corners[0] = jnp.where(lane // 2 == place, value, corners[0])

    for f in range(fields):
        pack_edge([tracers[f * pairs + k] for k in range(pairs)], f)
    pack_edge([cx[k] for k in range(pairs)], fields)
    pack_edge([cy[k] for k in range(pairs)], fields + 1)
    corner[...] = corners[0]
    courant = one_row([cx[k] for k in range(pairs)], 0, 1)
    courant += one_row([cy[k] for k in range(pairs)], 0, 1)
    for k, value in enumerate(courant):
        south_rows[fields * half + k] = value


def cosine_sums(values):
    count = len(values)
    if count == 1:
        return values
    half = count // 2
    plus = [values[n] + values[count - 1 - n] for n in range(half)]
    minus = [
        (values[n] - values[count - 1 - n])
        * (0.5 / math.cos(math.pi * (2 * n + 1) / (2 * count)))
        for n in range(half)
    ]
    even = cosine_sums(plus)
    odd = cosine_sums(minus)
    result = []
    for k in range(half):
        result.append(even[k])
        result.append(odd[k] + odd[k + 1] if k + 1 < half else odd[k])
    return result


def cosine_series(values):
    count = len(values)
    if count == 1:
        return values
    half = count // 2
    odd_in = [values[2 * k + 1] + values[2 * k - 1] if k else values[1] for k in range(half)]
    even = cosine_series(values[0::2])
    odd = cosine_series(odd_in)
    odd = [
        odd[n] * (0.5 / math.cos(math.pi * (2 * n + 1) / (2 * count))) for n in range(half)
    ]
    return [even[n] + odd[n] for n in range(half)] + [
        even[n] - odd[n] for n in range(half - 1, -1, -1)
    ]


def prep_kernel(coeffs, profile, klass, target, decay, source, onehot):
    levels, pairs = decay.shape[:2]
    fields = profile.shape[0]
    tile = decay.shape[2:]
    rows, lanes = klass.shape
    sub, lane = iotas(tile)
    low = sub < rows
    kind = jnp.concatenate([klass[...], klass[...]], axis=0)
    is_two = kind == 2
    is_one = kind == 1

    def by_class(which, f):
        return jnp.where(
            is_two,
            coeffs[which, 2, f] * 0.25,
            jnp.where(is_one, coeffs[which, 1, f] * 0.5, coeffs[which, 0, f]),
        )

    for p in range(pairs):
        f1 = 2 * p
        f2 = min(2 * p + 1, fields - 1)
        diffusion = jnp.where(low, by_class(0, f1), by_class(0, f2))
        relax = jnp.where(low, by_class(1, f1), by_class(1, f2))
        waves = cosine_sums([jnp.where(low, profile[f1, l], profile[f2, l]) for l in range(levels)])
        for m in range(levels):
            rate = relax + diffusion * (2.0 - 2.0 * math.cos(math.pi * m / levels))
            once = 1.0 / (1.0 + rate)
            square = once * once
            twice = once + square
            steps = jnp.where(is_two, twice + twice * square, jnp.where(is_one, twice, once))
            steps = steps * ((1.0 if m == 0 else 2.0) / levels)
            decay[m, p] = steps * rate
            source[m, p] = steps * relax * waves[m]
    low_part = target[...] & (lanes - 1)
    slot, _ = iotas((lanes, lanes))
    for r in range(rows):
        hit = jnp.where(slot == low_part[r : r + 1], 1.0, 0.0)
        onehot[r * lanes : (r + 1) * lanes, :] = jnp.transpose(hit).astype(jnp.bfloat16)


def combine(coefs, center, east, west, north, south):
    return (
        coefs[0] * center
        + (coefs[1] * east + coefs[2] * west)
        + (coefs[3] * north + coefs[4] * south)
    )


def coefficients(here_x, west_x, here_y, south_y):
    return (
        1.0
        - jnp.maximum(here_x, 0.0)
        + jnp.minimum(west_x, 0.0)
        - jnp.maximum(here_y, 0.0)
        + jnp.minimum(south_y, 0.0),
        jnp.maximum(-here_x, 0.0),
        jnp.maximum(west_x, 0.0),
        jnp.maximum(-here_y, 0.0),
        jnp.maximum(south_y, 0.0),
    )


def side_by_side(value, place):
    return jnp.where(place == 3, lane_roll(value, -2), value)


def beside(edge, edge_west, edge_east, slot, place):
    from_east = (place == 2) | (place == 3)
    from_west = (place == 4) | (place == 5)
    return jnp.where(
        from_east, edge_east[slot], jnp.where(from_west, edge_west[slot], edge[slot])
    )


def spread(value, levels):
    lanes = value.shape[1]
    rows = value.shape[0] // 2
    group = lanes // levels
    sub, lane = iotas(value.shape)
    value = side_by_side(value, lane % group)
    value = jnp.where(sub < rows, value, sub_roll(lane_roll(value, -group), rows))
    return [lane_roll(value, -(2 * group * k + 3)) for k in range(levels // 2)]


def shift_kernel(levels, tracers, edge, edge_west, edge_east, east, west):
    pairs = levels // 2
    tile = tracers.shape[1:]
    lanes = tile[1]
    lane = iotas(tile)[1]
    place = lane % (lanes // levels)
    for f in range(tracers.shape[0] // pairs):
        for k, sides in enumerate(spread(beside(edge, edge_west, edge_east, f, place), levels)):
            own = tracers[f * pairs + k]
            east[f * pairs + k] = jnp.where(lane == lanes - 1, sides, lane_roll(own, -1))
            west[f * pairs + k] = jnp.where(lane == 0, sides, lane_roll(own, 1))


def next_kernel(levels, cx, edge, edge_west, edge_east, next_sides, west_x, sides_y):
    pairs = levels // 2
    fields = next_sides.shape[0] // pairs
    tile = cx.shape[1:]
    rows = tile[0] // 2
    sub, lane = iotas(tile)
    place = lane % (tile[1] // levels)

    def own_rows(slot):
        value = beside(edge, edge_west, edge_east, slot, place)
        return jnp.where(sub < rows, value, 0.0)

    edge_x = own_rows(fields)
    edge_y = own_rows(fields + 1)
    coefs = coefficients(edge_x, lane_roll(edge_x, 1), edge_y, sub_roll(edge_y, 1))
    for k, sides in enumerate(spread(edge_x, levels)):
        west_x[k] = jnp.where(lane == 0, sides, lane_roll(cx[k], 1))
    for k, sides in enumerate(spread(edge_y, levels)):
        sides_y[k] = sides
    for f in range(fields):
        raw = own_rows(f)
        moved = combine(
            coefs,
            raw,
            lane_roll(raw, -1),
            lane_roll(raw, 1),
            sub_roll(raw, -1),
            sub_roll(raw, 1),
        )
        for k, sides in enumerate(spread(moved, levels)):
            next_sides[f * pairs + k] = sides


def transport_and_solve(
    fields,
    levels,
    tracers,
    cx,
    cy,
    from_south,
    from_north,
    east,
    west,
    next_sides,
    west_x,
    sides_y,
    corner_sw,
    corner_se,
    corner_nw,
    corner_ne,
    decay,
    source,
    state,
    own_coefs,
    halo_coefs,
):
    pairs = levels // 2
    half = pairs // 2
    tile = tracers.shape[1:]
    rows = tile[0] // 2
    lanes = tile[1]
    group = lanes // levels
    sub, lane = iotas(tile)
    local = sub % rows
    low = sub < rows
    first_lane = lane == 0
    last_lane = lane == lanes - 1
    odd_sub = sub % 2 == 1
    bottom = local == 0
    top = local == rows - 1
    in_first = bottom | top

    even_lane = lane % 2 == 0
    dense = jnp.where(
        odd_sub,
        jnp.where(even_lane, lane_roll(corner_se[...], -1), lane_roll(corner_sw[...], 1)),
        jnp.where(even_lane, lane_roll(corner_ne[...], -1), lane_roll(corner_nw[...], 1)),
    )

    def corner(slot, k):
        return pltpu.roll(dense, lanes - 2 * (slot * half + k) - 1, 1)


    def turned(value):
        up, down = sub_roll(value, rows - 1), sub_roll(value, 1 - rows)
        return ((up, down), (down, up))

    def inner_rows(first, second):
        (first_up, first_down), _ = turned(first)
        (second_up, second_down), _ = turned(second)
        return (
            jnp.where(in_first, first_up, second_down),
            jnp.where(in_first, first_down, second_up),
        )

    base = fields * half
    count = pairs // rows
    for k in range(half):
        quad, t = 2 * k // rows, 2 * k % rows
        packed_south = from_south[base + half + quad]
        packed_north = from_north[base + quad]
        packed_north_y = from_north[base + count + quad]
        message_y = from_south[base + k]
        south_x = jnp.where(in_first, sub_roll(packed_south, t), sub_roll(packed_south, 3 + t))
        north_x = jnp.where(in_first, sub_roll(packed_north, -t), sub_roll(packed_north, 5 - t))
        north_y = jnp.where(
            in_first, sub_roll(packed_north_y, -t), sub_roll(packed_north_y, 5 - t)
        )
        halo_x = jnp.where(odd_sub, south_x, north_x)
        halo_y = jnp.where(odd_sub, message_y, north_y)
        halo_west = jnp.where(first_lane, corner(fields, k), lane_roll(halo_x, 1))
        _, inner_top = inner_rows(cy[2 * k], cy[2 * k + 1])
        halo_south = jnp.where(odd_sub, sub_roll(message_y, 1), inner_top)
        for c, value in enumerate(coefficients(halo_x, halo_west, halo_y, halo_south)):
            halo_coefs[k, c] = value
        places = turned(message_y)
        edge_places = turned(corner(fields + 1, k))
        for i in range(2):
            j = 2 * k + i
            south_y = jnp.where(bottom, places[i][1], sub_roll(cy[j], 1))
            for c, value in enumerate(coefficients(cx[j], west_x[j], cy[j], south_y)):
                own_coefs[j, c] = value
            south_face = edge_places[i][1]
            own_coefs[j, 5] = jnp.where(bottom, jnp.minimum(south_face, 0.0), 0.0)
            own_coefs[j, 6] = jnp.where(
                bottom,
                jnp.maximum(south_face, 0.0),
                jnp.where(top, jnp.maximum(-sides_y[j], 0.0), 0.0),
            )

    def advect(f, k, own_set, halo_set):
        message_south = from_south[f * half + k]
        message_north = from_north[f * half + k]
        slots = (f * pairs + 2 * k, f * pairs + 2 * k + 1)
        own = [tracers[slot] for slot in slots]
        own_east = [east[slot] for slot in slots]
        own_west = [west[slot] for slot in slots]
        sides = corner(f, k)
        halo = jnp.where(odd_sub, message_south, message_north)
        inner_bottom, inner_top = inner_rows(*own)
        next_halo = combine(
            halo_set,
            halo,
            jnp.where(last_lane, sides, lane_roll(halo, -1)),
            jnp.where(first_lane, sides, lane_roll(halo, 1)),
            jnp.where(odd_sub, inner_bottom, sub_roll(message_north, -1)),
            jnp.where(odd_sub, sub_roll(message_south, 1), inner_top),
        )
        places, next_places, side_places = turned(halo), turned(next_halo), turned(sides)
        results = []
        for i in range(2):
            north, south = places[i]
            once = combine(
                own_set[i],
                own[i],
                own_east[i],
                own_west[i],
                jnp.where(top, north, sub_roll(own[i], -1)),
                jnp.where(bottom, south, sub_roll(own[i], 1)),
            )
            side_north, side_south = side_places[i]
            next_column = (
                next_sides[slots[i]]
                + own_set[i][5] * jnp.where(first_lane, own_west[i], own_east[i])
                + own_set[i][6] * jnp.where(bottom, side_south, side_north)
            )
            north, south = next_places[i]
            results.append(
                combine(
                    own_set[i],
                    once,
                    jnp.where(last_lane, next_column, lane_roll(once, -1)),
                    jnp.where(first_lane, next_column, lane_roll(once, 1)),
                    jnp.where(top, north, sub_roll(once, -1)),
                    jnp.where(bottom, south, sub_roll(once, 1)),
                )
            )
        return results

    def transport(p):
        f1 = 2 * p
        f2 = jnp.minimum(f1 + 1, fields - 1)
        columns = []
        for k in range(half):
            own_set = [[own_coefs[2 * k + i, c] for c in range(7)] for i in range(2)]
            halo_set = [halo_coefs[k, c] for c in range(5)]
            for one, two in zip(
                advect(f1, k, own_set, halo_set), advect(f2, k, own_set, halo_set)
            ):
                columns.append(jnp.where(low, one, sub_roll(two, rows)))
                columns.append(jnp.where(low, sub_roll(one, rows), two))
        return tuple(columns)

    def solve(p, columns):
        f1 = 2 * p
        f2 = jnp.minimum(f1 + 1, fields - 1)
        waves = cosine_sums(columns)
        change = cosine_series([source[m, p] - decay[m, p] * waves[m] for m in range(levels)])
        square = change[0] * change[0]
        for l in range(1, levels):
            square = square + change[l] * change[l]
        for k in range(pairs):
            even, odd = (columns[l] + change[l] for l in (2 * k, 2 * k + 1))
            state[f1 * pairs + k] = jnp.where(low, even, sub_roll(odd, rows))
            state[f2 * pairs + k] = jnp.where(low, sub_roll(even, rows), odd)
        return jnp.where(low | (f1 + 1 < fields), square, 0.0)

    def pair_step(p, carried):
        total, columns = carried
        following = transport(p)
        return total + solve(p - 1, columns), following

    field_pairs = (fields + 1) // 2
    total, columns = lax.fori_loop(
        1, field_pairs, pair_step, (jnp.zeros(tile, F32), transport(0))
    )
    return total + solve(field_pairs - 1, columns)


def main_kernel(fields, levels, *refs):
    inputs, (target, onehot), (state, placed), coefs = refs[:16], refs[16:18], refs[18:20], refs[20:]
    rows, lanes = target.shape
    total = transport_and_solve(fields, levels, *inputs, state, *coefs)

    heat = (total + sub_roll(total, rows)) * (1.0 / (fields * levels))
    first = heat.astype(jnp.bfloat16).astype(F32)
    rest = heat - first
    second = rest.astype(jnp.bfloat16).astype(F32)
    third = rest - second
    spans = placed.shape[0]
    slot_row, _ = iotas((spans, lanes))
    high = lax.shift_right_logical(target[...], lanes.bit_length() - 1)
    hits = [slot_row == high[r : r + 1] for r in range(rows)]
    left = jnp.concatenate(
        [
            jnp.concatenate(
                [
                    jnp.where(hits[r], part[r : r + 1], 0.0).astype(jnp.bfloat16)
                    for r in range(rows)
                ],
                axis=1,
            )
            for part in (first, second, third)
        ],
        axis=0,
    )
    result = jnp.dot(left, onehot[...], preferred_element_type=F32)
    placed[...] = result[:spans] + result[spans : 2 * spans] + result[2 * spans :]


def finish_kernel(parts, state, total_out, state_out, total, semaphores):
    copy_state = pltpu.make_async_copy(state, state_out, semaphores.at[0])
    copy_state.start()
    value = parts[0]
    for i in range(1, parts.shape[0]):
        value = value + parts[i]
    total[...] = value
    copy_total = pltpu.make_async_copy(total, total_out, semaphores.at[1])
    copy_total.start()
    copy_state.wait()
    copy_total.wait()


def body(tracers, courant_x, courant_y, physics_ref, class_coeffs, span_target, cloud_class):
    fields, levels, rows, cols = tracers.shape
    wide = lax.axis_size("wide")
    narrow = lax.axis_size("narrow")
    pairs = levels // 2
    half = pairs // 2
    tile = (2 * rows, cols)
    field_pairs = (fields + 1) // 2
    flat = tracers.reshape(fields * pairs, *tile)
    cx = courant_x.reshape(pairs, *tile)
    cy = courant_y.reshape(pairs, *tile)
    quads = pairs // rows

    def array(*shape, dtype=F32):
        return jax.ShapeDtypeStruct(shape, dtype)

    flat, cx, cy, north = pl.pallas_call(
        functools.partial(pack_north_kernel, levels),
        out_shape=(
            array(fields * pairs, *tile),
            array(pairs, *tile),
            array(pairs, *tile),
            array(fields * half + half + quads, *tile),
        ),
        in_specs=[HBM] * 3,
        out_specs=[VMEM] * 4,
        scratch_shapes=[pltpu.SemaphoreType.DMA((3,))],
        compiler_params=PARAMS,
    )(*(pltpu.with_memory_space_constraint(x, pltpu.HBM) for x in (flat, cx, cy)))
    edge, corner, south = pl.pallas_call(
        functools.partial(pack_edges_kernel, levels),
        out_shape=(
            array(fields + 2, *tile),
            array(*tile),
            array(fields * half + 2 * quads, *tile),
        ),
        in_specs=[VMEM] * 3,
        out_specs=[VMEM] * 3,
        compiler_params=PARAMS,
    )(flat, cx, cy)

    def send(value, up, right):
        pairs_ = []
        for w in range(wide):
            for n in range(narrow):
                to = ((w + up) % wide) * narrow + (n + right) % narrow
                pairs_.append((w * narrow + n, to))
        return lax.ppermute(value, ("wide", "narrow"), pairs_)

    def to_both_sides(value, up):
        from_west = send(value, up, 1)
        from_east = from_west if narrow == 2 else send(value, up, -1)
        return from_west, from_east

    from_south = send(north, 1, 0)
    from_north = send(south, -1, 0)
    edge_west, edge_east = to_both_sides(edge, 0)
    corner_sw, corner_se = to_both_sides(corner, 1)
    corner_nw, corner_ne = to_both_sides(corner, -1)

    decay, source, onehot = pl.pallas_call(
        prep_kernel,
        out_shape=(array(levels, field_pairs, *tile),) * 2
        + (array(rows * cols, cols, dtype=jnp.bfloat16),),
        in_specs=[SMEM, SMEM, VMEM, VMEM],
        out_specs=[VMEM] * 3,
        cost_estimate=pl.CostEstimate(flops=4000000, bytes_accessed=2000000, transcendentals=0),
        compiler_params=PARAMS,
    )(class_coeffs, physics_ref, cloud_class, span_target)

    shifted = pl.pallas_call(
        functools.partial(shift_kernel, levels),
        out_shape=(array(fields * pairs, *tile),) * 2,
        in_specs=[VMEM] * 4,
        out_specs=[VMEM] * 2,
        compiler_params=PARAMS,
    )(flat, edge, edge_west, edge_east)
    edge_columns = pl.pallas_call(
        functools.partial(next_kernel, levels),
        out_shape=(array(fields * pairs, *tile),) + (array(pairs, *tile),) * 2,
        in_specs=[VMEM] * 4,
        out_specs=[VMEM] * 3,
        compiler_params=PARAMS,
    )(cx, edge, edge_west, edge_east)
    state, placed = pl.pallas_call(
        functools.partial(main_kernel, fields, levels),
        out_shape=(array(fields * pairs, *tile), array(wide * rows, cols)),
        in_specs=[VMEM] * 18,
        out_specs=[VMEM] * 2,
        scratch_shapes=[
            pltpu.VMEM((pairs, 7) + tile, F32),
            pltpu.VMEM((half, 5) + tile, F32),
        ],
        compiler_params=PARAMS,
    )(
        flat,
        cx,
        cy,
        from_south,
        from_north,
        *shifted,
        *edge_columns,
        corner_sw,
        corner_se,
        corner_nw,
        corner_ne,
        decay,
        source,
        span_target,
        onehot,
    )
    received = lax.all_to_all(
        placed.reshape(wide, rows, cols), "wide", split_axis=0, concat_axis=0, tiled=True
    )
    span_diag, state = pl.pallas_call(
        finish_kernel,
        out_shape=(array(rows, cols), array(fields * pairs, *tile)),
        in_specs=[VMEM] * 2,
        out_specs=[HBM] * 2,
        scratch_shapes=[pltpu.VMEM((rows, cols), F32), pltpu.SemaphoreType.DMA((2,))],
        compiler_params=PARAMS,
    )(received, state)
    return state.reshape(fields, levels, rows, cols), span_diag


def solution(mesh):
    return jax.shard_map(
        body,
        mesh=mesh,
        in_specs=(
            P(None, None, "wide", "narrow"),
            P(None, "wide", "narrow"),
            P(None, "wide", "narrow"),
            P(),
            P(),
            P("wide", "narrow"),
            P("wide", "narrow"),
        ),
        out_specs=(P(None, None, "wide", "narrow"), P("wide", "narrow")),
        check_vma=False,
    )
```

profile of v0, /device:TPU:0, one launch (start us, length us, event | category | flops | bytes accessed | tf_op | source)
XLA Modules:
  0.0 32.1 jit_solution(1583537845741290532)
XLA Ops:
  0.6 1.1 %shard_map.86 = (f32[104,8,128]{2,1,0:T(8,128)S(1)}, f32[8,8,128]{2,1,0:T(8,128)S(1)}, f32[8,8,128]{2,1,0:T(8,128)S(1)}, f32[58,8,128]{2,1,0:T(8,128)S(1)}) custom-call(f32[104,8,128]{2,1,0:T(8,128)} %bitcast.6, f32[8,8,128]{2,1,0:T(8,128)} %bitcast.7, f32[8,8,128]{2,1,0:T(8,128)} %bitcast.8), custom_call_target="tpu_custom_call" | custom-call | tf_op jit(solution)/shard_map/pallas_call | solution.py:528
  1.7 3.0 %collective-permute-start = (f32[58,8,128]{2,1,0:T(8,128)S(1)}, f32[58,8,128]{2,1,0:T(8,128)S(1)}, u32[]{:S(2)}, u32[]{:S(2)}) collective-permute-start(f32[58,8,128]{2,1,0:T(8,128)S(1)} %get-tuple-element.24), channel_id=1, source_target_pairs={{0,2},{1,3},{2,4},{3,5},{4,6},{5,7},{6,8},{7,9},{8,10},{9,11},{10,... | collective-permute-start | bytes 712712 | tf_op jit(solution)/shard_map/ppermute | solution.py:559
  4.7 0.0 copy-start.3
  4.7 0.6 %shard_map.87 = (f32[15,8,128]{2,1,0:T(8,128)S(1)}, f32[8,128]{1,0:T(8,128)S(1)}, f32[56,8,128]{2,1,0:T(8,128)S(1)}) custom-call(f32[104,8,128]{2,1,0:T(8,128)S(1)} %get-tuple-element.21.tracers.refs_0_, f32[8,8,128]{2,1,0:T(8,128)S(1)} %get-tuple-element.22.cx.refs_1_, f32[8,8,128]{2,1,0:T(8,128)S(1)} %get-tuple-element.23.cy.refs_2_), custom_call_target="tpu_custom_call" | custom-call | tf_op jit(solution)/shard_map/pallas_call | solution.py:541
  5.3 0.0 copy-start
  5.3 4.1 %collective-permute-start.1 = (f32[56,8,128]{2,1,0:T(8,128)S(1)}, f32[56,8,128]{2,1,0:T(8,128)S(1)}, u32[]{:S(2)}, u32[]{:S(2)}) collective-permute-start(f32[56,8,128]{2,1,0:T(8,128)S(1)} %get-tuple-element.25), channel_id=1, source_target_pairs={{0,30},{1,31},{2,0},{3,1},{4,2},{5,3},{6,4},{7,5},{8,6},{9,7},{10,... | collective-permute-start | bytes 688136 | tf_op jit(solution)/shard_map/ppermute | solution.py:559
  9.4 0.0 collective-permute-start.2
  9.4 2.1 %collective-permute-start.4 = (f32[8,128]{1,0:T(8,128)S(1)}, f32[8,128]{1,0:T(8,128)S(1)}, u32[]{:S(2)}, u32[]{:S(2)}) collective-permute-start(f32[8,128]{1,0:T(8,128)S(1)} %get-tuple-element.32), channel_id=1, source_target_pairs={{0,31},{1,30},{2,1},{3,0},{4,3},{5,2},{6,5},{7,4},{8,7},{9,6},{10,... | collective-permute-start | bytes 12296 | tf_op jit(solution)/shard_map/ppermute | solution.py:559
  11.5 0.0 collective-permute-start.3
  11.5 0.0 copy-done.3
  11.5 0.0 copy-done
  11.5 0.0 copy-done.1
  11.6 0.0 copy-done.2
  11.6 1.2 %shard_map.90 = (f32[16,7,8,128]{3,2,1,0:T(8,128)S(1)}, f32[16,7,8,128]{3,2,1,0:T(8,128)S(1)}, bf16[512,128]{1,0:T(8,128)(2,1)S(1)}) custom-call(f32[2,3,13]{2,1,0:T(4,128)S(1)} %copy.9.coeffs, f32[13,16]{1,0:T(8,128)S(1)} %copy-done, s32[4,128]{1,0:T(4,128)S(1)} %copy-done.2, s32[4,128]{1,0:T(4,128)S(1)} %copy-done.1), custom_call_target="tpu_custom_call" | custom-call | flops 4000000 | bytes 2000000 | tf_op jit(solution)/shard_map/pallas_call | solution.py:572
  12.8 0.0 collective-permute-done.2.edge_west.edge_east
  12.8 0.4 %shard_map.89 = (f32[104,8,128]{2,1,0:T(8,128)S(1)}, f32[8,8,128]{2,1,0:T(8,128)S(1)}, f32[8,8,128]{2,1,0:T(8,128)S(1)}) custom-call(f32[8,8,128]{2,1,0:T(8,128)S(1)} %get-tuple-element.22.cx.refs_1_, f32[15,8,128]{2,1,0:T(8,128)S(1)} %get-tuple-element.26.edge, f32[15,8,128]{2,1,0:T(8,128)S(1)} %collective-permute-done.2.edge_west.edge_east, ...), custom_call_target="tpu_custom_call" | custom-call | tf_op jit(solution)/shard_map/pallas_call | solution.py:589
  13.2 1.2 %shard_map.88 = (f32[104,8,128]{2,1,0:T(8,128)S(1)}, f32[104,8,128]{2,1,0:T(8,128)S(1)}) custom-call(f32[104,8,128]{2,1,0:T(8,128)S(1)} %get-tuple-element.21.tracers.refs_0_, f32[15,8,128]{2,1,0:T(8,128)S(1)} %get-tuple-element.26.edge, f32[15,8,128]{2,1,0:T(8,128)S(1)} %collective-permute-done.2.edge_west.edge_east, ...), custom_call_target="tpu_custom_call" | custom-call | tf_op jit(solution)/shard_map/pallas_call | solution.py:582
  14.4 1.1 %collective-permute-done.4.refs_12_.refs_13_ = f32[8,128]{1,0:T(8,128)S(1)} collective-permute-done((f32[8,128]{1,0:T(8,128)S(1)}, f32[8,128]{1,0:T(8,128)S(1)}, u32[]{:S(2)}, u32[]{:S(2)}) %collective-permute-start.4) | collective-permute-done | bytes 4128 | tf_op jit(solution)/shard_map/ppermute | solution.py:559
  15.5 2.7 %collective-permute-done.3.refs_10_.refs_11_ = f32[8,128]{1,0:T(8,128)S(1)} collective-permute-done((f32[8,128]{1,0:T(8,128)S(1)}, f32[8,128]{1,0:T(8,128)S(1)}, u32[]{:S(2)}, u32[]{:S(2)}) %collective-permute-start.3) | collective-permute-done | bytes 4128 | tf_op jit(solution)/shard_map/ppermute | solution.py:559
  18.3 0.0 collective-permute-done.1.refs_4_
  18.3 0.0 collective-permute-done.refs_3_
  18.3 1.6 %shard_map.91 = (f32[104,8,128]{2,1,0:T(8,128)S(1)}, f32[64,128]{1,0:T(8,128)S(1)}) custom-call(f32[104,8,128]{2,1,0:T(8,128)S(1)} %get-tuple-element.21.tracers.refs_0_, f32[8,8,128]{2,1,0:T(8,128)S(1)} %get-tuple-element.22.cx.refs_1_, f32[8,8,128]{2,1,0:T(8,128)S(1)} %get-tuple-element.23.cy.refs_2_, f32[58,8,128]{2,1,0:T(8,128)S(1)} %collective-permute-done.refs_3_, ...), custom_call_target="tpu_custom_call" | custom-call | tf_op jit(solution)/shard_map/pallas_call | solution.py:596
  19.8 11.5 %all_to_all.5.parts = f32[16,4,128]{2,1,0:T(4,128)S(1)} all-to-all(f32[16,4,128]{2,1,0:T(4,128)S(1)} %bitcast.5), channel_id=1, replica_groups=mesh['wide'=16,'narrow'=2] {'wide'}, dimensions={0} | all-to-all | bytes 65536 | tf_op jit(solution)/shard_map/all_to_all | solution.py:623
  31.4 0.8 %shard_map.92 = (f32[4,128]{1,0:T(4,128)}, f32[104,8,128]{2,1,0:T(8,128)}) custom-call(f32[16,4,128]{2,1,0:T(4,128)S(1)} %all_to_all.5.parts, f32[104,8,128]{2,1,0:T(8,128)S(1)} %get-tuple-element.37.state), custom_call_target="tpu_custom_call" | custom-call | tf_op jit(solution)/shard_map/pallas_call | solution.py:626
  (3 shorter events, 0.0 us)
Async XLA Ops:
  1.7 16.6 %collective-permute-start = (f32[58,8,128]{2,1,0:T(8,128)S(1)}, f32[58,8,128]{2,1,0:T(8,128)S(1)}, u32[]{:S(2)}, u32[]{:S(2)}) collective-permute-start(f32[58,8,128]{2,1,0:T(8,128)S(1)} %get-tuple-element.24), channel_id=1, source_target_pairs={{0,2},{1,3},{2,4},{3,5},{4,6},{5,7},{6,8},{7,9},{8,10},{9,11},{10,... | collective-permute-start | bytes 712712 | tf_op jit(solution)/shard_map/ppermute | solution.py:559
  4.7 6.8 %copy-start.3 = (f32[2,3,13]{2,0,1:T(2,128)S(1)}, f32[2,3,13]{2,0,1:T(2,128)}, u32[]{:S(2)}) copy-start(f32[2,3,13]{2,0,1:T(2,128)} %param.11) | copy-start | bytes 940
  5.3 6.2 %copy-start = (f32[13,16]{1,0:T(8,128)S(1)}, f32[13,16]{1,0:T(8,128)}, u32[]{:S(2)}) copy-start(f32[13,16]{1,0:T(8,128)} %profile.1) | copy-start | bytes 2500
  5.3 12.9 %collective-permute-start.1 = (f32[56,8,128]{2,1,0:T(8,128)S(1)}, f32[56,8,128]{2,1,0:T(8,128)S(1)}, u32[]{:S(2)}, u32[]{:S(2)}) collective-permute-start(f32[56,8,128]{2,1,0:T(8,128)S(1)} %get-tuple-element.25), channel_id=1, source_target_pairs={{0,30},{1,31},{2,0},{3,1},{4,2},{5,3},{6,4},{7,5},{8,6},{9,7},{10,... | collective-permute-start | bytes 688136 | tf_op jit(solution)/shard_map/ppermute | solution.py:559
  9.4 3.4 %collective-permute-start.2 = (f32[15,8,128]{2,1,0:T(8,128)S(1)}, f32[15,8,128]{2,1,0:T(8,128)S(1)}, u32[]{:S(2)}, u32[]{:S(2)}) collective-permute-start(f32[15,8,128]{2,1,0:T(8,128)S(1)} %get-tuple-element.26.edge), channel_id=1, source_target_pairs={{0,1},{1,0},{2,3},{3,2},{4,5},{5,4},{6,7},{7,6},{8,9},{9,8},{10,11... | collective-permute-start | bytes 184328 | tf_op jit(solution)/shard_map/ppermute | solution.py:559
  9.4 2.1 %copy-start.1 = (s32[4,128]{1,0:T(4,128)S(1)}, s32[4,128]{1,0:T(4,128)}, u32[]{:S(2)}) copy-start(s32[4,128]{1,0:T(4,128)} %refs_16_.1) | copy-start | bytes 6148
  9.4 2.1 %copy-start.2 = (s32[4,128]{1,0:T(4,128)S(1)}, s32[4,128]{1,0:T(4,128)}, u32[]{:S(2)}) copy-start(s32[4,128]{1,0:T(4,128)} %klass.1) | copy-start | bytes 6148
  9.4 6.1 %collective-permute-start.4 = (f32[8,128]{1,0:T(8,128)S(1)}, f32[8,128]{1,0:T(8,128)S(1)}, u32[]{:S(2)}, u32[]{:S(2)}) collective-permute-start(f32[8,128]{1,0:T(8,128)S(1)} %get-tuple-element.32), channel_id=1, source_target_pairs={{0,31},{1,30},{2,1},{3,0},{4,3},{5,2},{6,5},{7,4},{8,7},{9,6},{10,... | collective-permute-start | bytes 12296 | tf_op jit(solution)/shard_map/ppermute | solution.py:559
  11.5 6.7 %collective-permute-start.3 = (f32[8,128]{1,0:T(8,128)S(1)}, f32[8,128]{1,0:T(8,128)S(1)}, u32[]{:S(2)}, u32[]{:S(2)}) collective-permute-start(f32[8,128]{1,0:T(8,128)S(1)} %get-tuple-element.32), channel_id=1, source_target_pairs={{0,3},{1,2},{2,5},{3,4},{4,7},{5,6},{6,9},{7,8},{8,11},{9,10},{10,... | collective-permute-start | bytes 12296 | tf_op jit(solution)/shard_map/ppermute | solution.py:559
where the time goes:
time: 32.3 us; the launch traced here: 32.1 us
  blocking collectives  11.5 us (36%)
  starting transfers between devices  9.18 us (28%)
  Pallas kernels  6.88 us (21%)
  waiting for transfers between devices  3.83 us (12%)
  between operations  0.71 us (2%)
    all_to_all x1, blocking collectives, body(): lax.all_to_all(placed.reshape(wide, rows, cols), 'wide', split_axis=0, co...  11.5 us
    ppermute x5, starting transfers between devices, send(): return lax.ppermute(value, ('wide', 'narrow'), pairs_)  9.18 us
    ppermute x5, waiting for transfers between devices, send(): return lax.ppermute(value, ('wide', 'narrow'), pairs_)  3.83 us
    pallas_call x1, Pallas kernels, body(): pl.pallas_call(functools.partial(main_kernel, fields, levels), out_shape=...  1.57 us
    pallas_call x1, Pallas kernels, body(): pl.pallas_call(prep_kernel, out_shape=(array(levels, field_pairs, *tile),...  1.23 us
    pallas_call x1, Pallas kernels, body(): pl.pallas_call(functools.partial(shift_kernel, levels), out_shape=(array(...  1.22 us
    pallas_call x1, Pallas kernels, body(): pl.pallas_call(functools.partial(pack_north_kernel, levels), out_shape=(a...  1.07 us
    pallas_call x1, Pallas kernels, body(): pl.pallas_call(finish_kernel, out_shape=(array(rows, cols), array(fields...  0.78 us
  transfers between devices with their start and end apart: 5, of which 2 were waited for; matrix products, arithmetic and copies ran while one was open for 0% of the time, Pallas kernels for 11%

commit v1 on v0

--- a/solution.py
+++ b/solution.py
@@ -41,6 +41,20 @@
             )
         packed.append(total)
     return packed
+
+
+def inner_flux(value, courant):
+    return jnp.maximum(courant, 0.0) * value + jnp.minimum(courant, 0.0) * sub_roll(value, -1)
+
+
+def northward_rows(value, courant):
+    local = iotas(value.shape)[0] % (value.shape[0] // 2)
+    return jnp.where(local == 2, inner_flux(value, courant), value)
+
+
+def southward_rows(value, courant):
+    local = iotas(value.shape)[0] % (value.shape[0] // 2)
+    return jnp.where(local == 1, sub_roll(-inner_flux(value, courant), 1), value)
 
 
 def pack_north_kernel(levels, tracers_in, cx_in, cy_in, tracers, cx, cy, north, semaphores):
@@ -60,13 +74,14 @@
     fields = tracers.shape[0] // pairs
     for f in range(fields):
         for k in range(half):
-            one, two = tracers[f * pairs + 2 * k], tracers[f * pairs + 2 * k + 1]
+            one, two = (
+                northward_rows(tracers[f * pairs + j], cy[j]) for j in (2 * k, 2 * k + 1)
+            )
             north[f * half + k] = jnp.where(upper, one, sub_roll(two, 2))
-    base = fields * half
-    for k in range(half):
-        north[base + k] = jnp.where(upper, cy[2 * k], sub_roll(cy[2 * k + 1], 2))
-    for k, value in enumerate(one_row([cx[k] for k in range(pairs)], rows - 1, -1)):
-        north[base + half + k] = value
+    courant = one_row([cx[k] for k in range(pairs)], rows - 1, -1)
+    courant += one_row([cy[k] for k in range(pairs)], rows - 1, -1)
+    for k, value in enumerate(courant):
+        north[fields * half + k] = value
 
 
 def pack_edges_kernel(levels, tracers, cx, cy, edge, corner, south_rows):
@@ -98,7 +113,9 @@
             north = jnp.where(upper, one, sub_roll(two, 2))
             south = jnp.where(upper, sub_roll(two, -2), one)
             if slot < fields:
-                south_rows[place] = south
+                first = southward_rows(one, cy[2 * k])
+                second = southward_rows(two, cy[2 * k + 1])
+                south_rows[place] = jnp.where(upper, sub_roll(second, -2), first)
             value = lane_roll(jnp.where(odd_sub, north, south), 2 * place + 1)
             corners[0] = jnp.where(lane // 2 == place, value, corners[0])
 
@@ -107,9 +124,7 @@
     pack_edge([cx[k] for k in range(pairs)], fields)
     pack_edge([cy[k] for k in range(pairs)], fields + 1)
     corner[...] = corners[0]
-    courant = one_row([cx[k] for k in range(pairs)], 0, 1)
-    courant += one_row([cy[k] for k in range(pairs)], 0, 1)
-    for k, value in enumerate(courant):
+    for k, value in enumerate(one_row([cx[k] for k in range(pairs)], 0, 1)):
         south_rows[fields * half + k] = value
 
 
@@ -345,28 +360,33 @@
     count = pairs // rows
     for k in range(half):
         quad, t = 2 * k // rows, 2 * k % rows
-        packed_south = from_south[base + half + quad]
+        packed_south = from_south[base + quad]
+        packed_south_y = from_south[base + count + quad]
         packed_north = from_north[base + quad]
-        packed_north_y = from_north[base + count + quad]
-        message_y = from_south[base + k]
         south_x = jnp.where(in_first, sub_roll(packed_south, t), sub_roll(packed_south, 3 + t))
+        south_y = jnp.where(
+            in_first, sub_roll(packed_south_y, t), sub_roll(packed_south_y, 3 + t)
+        )
         north_x = jnp.where(in_first, sub_roll(packed_north, -t), sub_roll(packed_north, 5 - t))
-        north_y = jnp.where(
-            in_first, sub_roll(packed_north_y, -t), sub_roll(packed_north_y, 5 - t)
-        )
         halo_x = jnp.where(odd_sub, south_x, north_x)
-        halo_y = jnp.where(odd_sub, message_y, north_y)
         halo_west = jnp.where(first_lane, corner(fields, k), lane_roll(halo_x, 1))
         _, inner_top = inner_rows(cy[2 * k], cy[2 * k + 1])
-        halo_south = jnp.where(odd_sub, sub_roll(message_y, 1), inner_top)
-        for c, value in enumerate(coefficients(halo_x, halo_west, halo_y, halo_south)):
-            halo_coefs[k, c] = value
-        places = turned(message_y)
+        face = jnp.where(odd_sub, -south_y, inner_top)
+        halo_coefs[k, 0] = (
+            1.0
+            - jnp.maximum(halo_x, 0.0)
+            + jnp.minimum(halo_west, 0.0)
+            + jnp.minimum(face, 0.0)
+        )
+        halo_coefs[k, 1] = jnp.maximum(-halo_x, 0.0)
+        halo_coefs[k, 2] = jnp.maximum(halo_west, 0.0)
+        halo_coefs[k, 3] = jnp.maximum(face, 0.0)
+        places = turned(south_y)
         edge_places = turned(corner(fields + 1, k))
         for i in range(2):
             j = 2 * k + i
-            south_y = jnp.where(bottom, places[i][1], sub_roll(cy[j], 1))
-            for c, value in enumerate(coefficients(cx[j], west_x[j], cy[j], south_y)):
+            below = jnp.where(bottom, places[i][1], sub_roll(cy[j], 1))
+            for c, value in enumerate(coefficients(cx[j], west_x[j], cy[j], below)):
                 own_coefs[j, c] = value
             south_face = edge_places[i][1]
             own_coefs[j, 5] = jnp.where(bottom, jnp.minimum(south_face, 0.0), 0.0)
@@ -386,13 +406,14 @@
         sides = corner(f, k)
         halo = jnp.where(odd_sub, message_south, message_north)
         inner_bottom, inner_top = inner_rows(*own)
-        next_halo = combine(
-            halo_set,
-            halo,
-            jnp.where(last_lane, sides, lane_roll(halo, -1)),
-            jnp.where(first_lane, sides, lane_roll(halo, 1)),
-            jnp.where(odd_sub, inner_bottom, sub_roll(message_north, -1)),
-            jnp.where(odd_sub, sub_roll(message_south, 1), inner_top),
+        flux = jnp.where(odd_sub, sub_roll(message_south, 1), sub_roll(message_north, -1))
+        next_halo = (
+            halo_set[0] * halo
+            + (
+                halo_set[1] * jnp.where(last_lane, sides, lane_roll(halo, -1))
+                + halo_set[2] * jnp.where(first_lane, sides, lane_roll(halo, 1))
+            )
+            + (halo_set[3] * jnp.where(odd_sub, inner_bottom, inner_top) + flux)
         )
         places, next_places, side_places = turned(halo), turned(next_halo), turned(sides)
         results = []
@@ -431,7 +452,7 @@
         columns = []
         for k in range(half):
             own_set = [[own_coefs[2 * k + i, c] for c in range(7)] for i in range(2)]
-            halo_set = [halo_coefs[k, c] for c in range(5)]
+            halo_set = [halo_coefs[k, c] for c in range(4)]
             for one, two in zip(
                 advect(f1, k, own_set, halo_set), advect(f2, k, own_set, halo_set)
             ):
@@ -531,7 +552,7 @@
             array(fields * pairs, *tile),
             array(pairs, *tile),
             array(pairs, *tile),
-            array(fields * half + half + quads, *tile),
+            array(fields * half + 2 * quads, *tile),
         ),
         in_specs=[HBM] * 3,
         out_specs=[VMEM] * 4,
@@ -543,7 +564,7 @@
         out_shape=(
             array(fields + 2, *tile),
             array(*tile),
-            array(fields * half + 2 * quads, *tile),
+            array(fields * half + quads, *tile),
         ),
         in_specs=[VMEM] * 3,
         out_specs=[VMEM] * 3,
@@ -600,7 +621,7 @@
         out_specs=[VMEM] * 2,
         scratch_shapes=[
             pltpu.VMEM((pairs, 7) + tile, F32),
-            pltpu.VMEM((half, 5) + tile, F32),
+            pltpu.VMEM((half, 4) + tile, F32),
         ],
         compiler_params=PARAMS,
     )(

time: 32.3 us -> 32 us (level)
    all_to_all x1, blocking collectives: 11.5 us -> 11.2 us  [body(): lax.all_to_all(placed.reshape(wide, rows, cols), 'wide', split_axis=0, co...]
where the time goes in v1:
time: 32 us; the launch traced here: 31.9 us
  blocking collectives  11.2 us (35%)
  starting transfers between devices  9.18 us (29%)
  Pallas kernels  6.94 us (22%)
  waiting for transfers between devices  3.83 us (12%)
  between operations  0.71 us (2%)
    all_to_all x1, blocking collectives, body(): lax.all_to_all(placed.reshape(wide, rows, cols), 'wide', split_axis=0, co...  11.2 us
    ppermute x5, starting transfers between devices, send(): return lax.ppermute(value, ('wide', 'narrow'), pairs_)  9.18 us
    ppermute x5, waiting for transfers between devices, send(): return lax.ppermute(value, ('wide', 'narrow'), pairs_)  3.83 us
    pallas_call x1, Pallas kernels, body(): pl.pallas_call(functools.partial(main_kernel, fields, levels), out_shape=...  1.56 us
    pallas_call x1, Pallas kernels, body(): pl.pallas_call(prep_kernel, out_shape=(array(levels, field_pairs, *tile),...  1.23 us
    pallas_call x1, Pallas kernels, body(): pl.pallas_call(functools.partial(shift_kernel, levels), out_shape=(array(...  1.22 us
    pallas_call x1, Pallas kernels, body(): pl.pallas_call(functools.partial(pack_north_kernel, levels), out_shape=(a...  1.13 us
    pallas_call x1, Pallas kernels, body(): pl.pallas_call(finish_kernel, out_shape=(array(rows, cols), array(fields...  0.78 us
  transfers between devices with their start and end apart: 5, of which 2 were waited for; matrix products, arithmetic and copies ran while one was open for 0% of the time, Pallas kernels for 11%

profile of v1, /device:TPU:0, one launch (start us, length us, event | category | flops | bytes accessed | tf_op | source)
XLA Modules:
  0.0 31.9 jit_solution(14587058603248226602)
XLA Ops:
  0.6 1.1 %shard_map.86 = (f32[104,8,128]{2,1,0:T(8,128)S(1)}, f32[8,8,128]{2,1,0:T(8,128)S(1)}, f32[8,8,128]{2,1,0:T(8,128)S(1)}, f32[56,8,128]{2,1,0:T(8,128)S(1)}) custom-call(f32[104,8,128]{2,1,0:T(8,128)} %bitcast.6, f32[8,8,128]{2,1,0:T(8,128)} %bitcast.7, f32[8,8,128]{2,1,0:T(8,128)} %bitcast.8), custom_call_target="tpu_custom_call" | custom-call | tf_op jit(solution)/shard_map/pallas_call | solution.py:549
  1.8 3.0 %collective-permute-start = (f32[56,8,128]{2,1,0:T(8,128)S(1)}, f32[56,8,128]{2,1,0:T(8,128)S(1)}, u32[]{:S(2)}, u32[]{:S(2)}) collective-permute-start(f32[56,8,128]{2,1,0:T(8,128)S(1)} %get-tuple-element.24), channel_id=1, source_target_pairs={{0,2},{1,3},{2,4},{3,5},{4,6},{5,7},{6,8},{7,9},{8,10},{9,11},{10,... | collective-permute-start | bytes 688136 | tf_op jit(solution)/shard_map/ppermute | solution.py:580
  4.8 0.0 copy-start.3
  4.8 0.6 %shard_map.87 = (f32[15,8,128]{2,1,0:T(8,128)S(1)}, f32[8,128]{1,0:T(8,128)S(1)}, f32[54,8,128]{2,1,0:T(8,128)S(1)}) custom-call(f32[104,8,128]{2,1,0:T(8,128)S(1)} %get-tuple-element.21.tracers.refs_0_, f32[8,8,128]{2,1,0:T(8,128)S(1)} %get-tuple-element.22.cx.refs_1_, f32[8,8,128]{2,1,0:T(8,128)S(1)} %get-tuple-element.23.cy.refs_2_), custom_call_target="tpu_custom_call" | custom-call | tf_op jit(solution)/shard_map/pallas_call | solution.py:562
  5.4 0.0 copy-start
  5.4 4.1 %collective-permute-start.1 = (f32[54,8,128]{2,1,0:T(8,128)S(1)}, f32[54,8,128]{2,1,0:T(8,128)S(1)}, u32[]{:S(2)}, u32[]{:S(2)}) collective-permute-start(f32[54,8,128]{2,1,0:T(8,128)S(1)} %get-tuple-element.25), channel_id=1, source_target_pairs={{0,30},{1,31},{2,0},{3,1},{4,2},{5,3},{6,4},{7,5},{8,6},{9,7},{10,... | collective-permute-start | bytes 663560 | tf_op jit(solution)/shard_map/ppermute | solution.py:580
  9.5 0.0 collective-permute-start.2
  9.5 2.1 %collective-permute-start.4 = (f32[8,128]{1,0:T(8,128)S(1)}, f32[8,128]{1,0:T(8,128)S(1)}, u32[]{:S(2)}, u32[]{:S(2)}) collective-permute-start(f32[8,128]{1,0:T(8,128)S(1)} %get-tuple-element.32), channel_id=1, source_target_pairs={{0,31},{1,30},{2,1},{3,0},{4,3},{5,2},{6,5},{7,4},{8,7},{9,6},{10,... | collective-permute-start | bytes 12296 | tf_op jit(solution)/shard_map/ppermute | solution.py:580
  11.6 0.0 collective-permute-start.3
  11.6 0.0 copy-done.3
  11.6 0.0 copy-done
  11.6 0.0 copy-done.1
  11.6 0.0 copy-done.2
  11.6 1.2 %shard_map.90 = (f32[16,7,8,128]{3,2,1,0:T(8,128)S(1)}, f32[16,7,8,128]{3,2,1,0:T(8,128)S(1)}, bf16[512,128]{1,0:T(8,128)(2,1)S(1)}) custom-call(f32[2,3,13]{2,1,0:T(4,128)S(1)} %copy.9.coeffs, f32[13,16]{1,0:T(8,128)S(1)} %copy-done, s32[4,128]{1,0:T(4,128)S(1)} %copy-done.2, s32[4,128]{1,0:T(4,128)S(1)} %copy-done.1), custom_call_target="tpu_custom_call" | custom-call | flops 4000000 | bytes 2000000 | tf_op jit(solution)/shard_map/pallas_call | solution.py:593
  12.9 0.0 collective-permute-done.2.edge_west.edge_east
  12.9 0.4 %shard_map.89 = (f32[104,8,128]{2,1,0:T(8,128)S(1)}, f32[8,8,128]{2,1,0:T(8,128)S(1)}, f32[8,8,128]{2,1,0:T(8,128)S(1)}) custom-call(f32[8,8,128]{2,1,0:T(8,128)S(1)} %get-tuple-element.22.cx.refs_1_, f32[15,8,128]{2,1,0:T(8,128)S(1)} %get-tuple-element.26.edge, f32[15,8,128]{2,1,0:T(8,128)S(1)} %collective-permute-done.2.edge_west.edge_east, ...), custom_call_target="tpu_custom_call" | custom-call | tf_op jit(solution)/shard_map/pallas_call | solution.py:610
  13.3 1.2 %shard_map.88 = (f32[104,8,128]{2,1,0:T(8,128)S(1)}, f32[104,8,128]{2,1,0:T(8,128)S(1)}) custom-call(f32[104,8,128]{2,1,0:T(8,128)S(1)} %get-tuple-element.21.tracers.refs_0_, f32[15,8,128]{2,1,0:T(8,128)S(1)} %get-tuple-element.26.edge, f32[15,8,128]{2,1,0:T(8,128)S(1)} %collective-permute-done.2.edge_west.edge_east, ...), custom_call_target="tpu_custom_call" | custom-call | tf_op jit(solution)/shard_map/pallas_call | solution.py:603
  14.5 0.7 %collective-permute-done.4.refs_12_.refs_13_ = f32[8,128]{1,0:T(8,128)S(1)} collective-permute-done((f32[8,128]{1,0:T(8,128)S(1)}, f32[8,128]{1,0:T(8,128)S(1)}, u32[]{:S(2)}, u32[]{:S(2)}) %collective-permute-start.4) | collective-permute-done | bytes 4128 | tf_op jit(solution)/shard_map/ppermute | solution.py:580
  15.2 3.1 %collective-permute-done.3.refs_10_.refs_11_ = f32[8,128]{1,0:T(8,128)S(1)} collective-permute-done((f32[8,128]{1,0:T(8,128)S(1)}, f32[8,128]{1,0:T(8,128)S(1)}, u32[]{:S(2)}, u32[]{:S(2)}) %collective-permute-start.3) | collective-permute-done | bytes 4128 | tf_op jit(solution)/shard_map/ppermute | solution.py:580
  18.3 0.0 collective-permute-done.1.refs_4_
  18.3 0.0 collective-permute-done.refs_3_
  18.3 1.6 %shard_map.91 = (f32[104,8,128]{2,1,0:T(8,128)S(1)}, f32[64,128]{1,0:T(8,128)S(1)}) custom-call(f32[104,8,128]{2,1,0:T(8,128)S(1)} %get-tuple-element.21.tracers.refs_0_, f32[8,8,128]{2,1,0:T(8,128)S(1)} %get-tuple-element.22.cx.refs_1_, f32[8,8,128]{2,1,0:T(8,128)S(1)} %get-tuple-element.23.cy.refs_2_, f32[56,8,128]{2,1,0:T(8,128)S(1)} %collective-permute-done.refs_3_, ...), custom_call_target="tpu_custom_call" | custom-call | tf_op jit(solution)/shard_map/pallas_call | solution.py:617
  19.9 11.2 %all_to_all.5.parts = f32[16,4,128]{2,1,0:T(4,128)S(1)} all-to-all(f32[16,4,128]{2,1,0:T(4,128)S(1)} %bitcast.5), channel_id=1, replica_groups=mesh['wide'=16,'narrow'=2] {'wide'}, dimensions={0} | all-to-all | bytes 65536 | tf_op jit(solution)/shard_map/all_to_all | solution.py:644
  31.1 0.8 %shard_map.92 = (f32[4,128]{1,0:T(4,128)}, f32[104,8,128]{2,1,0:T(8,128)}) custom-call(f32[16,4,128]{2,1,0:T(4,128)S(1)} %all_to_all.5.parts, f32[104,8,128]{2,1,0:T(8,128)S(1)} %get-tuple-element.37.state), custom_call_target="tpu_custom_call" | custom-call | tf_op jit(solution)/shard_map/pallas_call | solution.py:647
  (3 shorter events, 0.0 us)
Async XLA Ops:
  1.8 16.6 %collective-permute-start = (f32[56,8,128]{2,1,0:T(8,128)S(1)}, f32[56,8,128]{2,1,0:T(8,128)S(1)}, u32[]{:S(2)}, u32[]{:S(2)}) collective-permute-start(f32[56,8,128]{2,1,0:T(8,128)S(1)} %get-tuple-element.24), channel_id=1, source_target_pairs={{0,2},{1,3},{2,4},{3,5},{4,6},{5,7},{6,8},{7,9},{8,10},{9,11},{10,... | collective-permute-start | bytes 688136 | tf_op jit(solution)/shard_map/ppermute | solution.py:580
  4.8 6.8 %copy-start.3 = (f32[2,3,13]{2,0,1:T(2,128)S(1)}, f32[2,3,13]{2,0,1:T(2,128)}, u32[]{:S(2)}) copy-start(f32[2,3,13]{2,0,1:T(2,128)} %param.11) | copy-start | bytes 940
  5.4 6.2 %copy-start = (f32[13,16]{1,0:T(8,128)S(1)}, f32[13,16]{1,0:T(8,128)}, u32[]{:S(2)}) copy-start(f32[13,16]{1,0:T(8,128)} %profile.1) | copy-start | bytes 2500
  5.4 12.9 %collective-permute-start.1 = (f32[54,8,128]{2,1,0:T(8,128)S(1)}, f32[54,8,128]{2,1,0:T(8,128)S(1)}, u32[]{:S(2)}, u32[]{:S(2)}) collective-permute-start(f32[54,8,128]{2,1,0:T(8,128)S(1)} %get-tuple-element.25), channel_id=1, source_target_pairs={{0,30},{1,31},{2,0},{3,1},{4,2},{5,3},{6,4},{7,5},{8,6},{9,7},{10,... | collective-permute-start | bytes 663560 | tf_op jit(solution)/shard_map/ppermute | solution.py:580
  9.5 3.4 %collective-permute-start.2 = (f32[15,8,128]{2,1,0:T(8,128)S(1)}, f32[15,8,128]{2,1,0:T(8,128)S(1)}, u32[]{:S(2)}, u32[]{:S(2)}) collective-permute-start(f32[15,8,128]{2,1,0:T(8,128)S(1)} %get-tuple-element.26.edge), channel_id=1, source_target_pairs={{0,1},{1,0},{2,3},{3,2},{4,5},{5,4},{6,7},{7,6},{8,9},{9,8},{10,11... | collective-permute-start | bytes 184328 | tf_op jit(solution)/shard_map/ppermute | solution.py:580
  9.5 2.1 %copy-start.1 = (s32[4,128]{1,0:T(4,128)S(1)}, s32[4,128]{1,0:T(4,128)}, u32[]{:S(2)}) copy-start(s32[4,128]{1,0:T(4,128)} %refs_16_.1) | copy-start | bytes 6148
  9.5 2.1 %copy-start.2 = (s32[4,128]{1,0:T(4,128)S(1)}, s32[4,128]{1,0:T(4,128)}, u32[]{:S(2)}) copy-start(s32[4,128]{1,0:T(4,128)} %klass.1) | copy-start | bytes 6148
  9.5 5.8 %collective-permute-start.4 = (f32[8,128]{1,0:T(8,128)S(1)}, f32[8,128]{1,0:T(8,128)S(1)}, u32[]{:S(2)}, u32[]{:S(2)}) collective-permute-start(f32[8,128]{1,0:T(8,128)S(1)} %get-tuple-element.32), channel_id=1, source_target_pairs={{0,31},{1,30},{2,1},{3,0},{4,3},{5,2},{6,5},{7,4},{8,7},{9,6},{10,... | collective-permute-start | bytes 12296 | tf_op jit(solution)/shard_map/ppermute | solution.py:580
  11.6 6.7 %collective-permute-start.3 = (f32[8,128]{1,0:T(8,128)S(1)}, f32[8,128]{1,0:T(8,128)S(1)}, u32[]{:S(2)}, u32[]{:S(2)}) collective-permute-start(f32[8,128]{1,0:T(8,128)S(1)} %get-tuple-element.32), channel_id=1, source_target_pairs={{0,3},{1,2},{2,5},{3,4},{4,7},{5,6},{6,9},{7,8},{8,11},{9,10},{10,... | collective-permute-start | bytes 12296 | tf_op jit(solution)/shard_map/ppermute | solution.py:580

commit v2 on v1

--- a/solution.py
+++ b/solution.py
@@ -294,6 +294,45 @@
             next_sides[f * pairs + k] = sides
 
 
+def turned(value):
+    rows = value.shape[0] // 2
+    up, down = sub_roll(value, rows - 1), sub_roll(value, 1 - rows)
+    return ((up, down), (down, up))
+
+
+def corner_kernel(
+    levels, sides_y, corner_sw, corner_se, corner_nw, corner_ne, corners, shares
+):
+    half = levels // 4
+    tile = corner_sw.shape
+    rows = tile[0] // 2
+    sub, lane = iotas(tile)
+    local = sub % rows
+    odd_sub = sub % 2 == 1
+    bottom = local == 0
+    top = local == rows - 1
+    even_lane = lane % 2 == 0
+    dense = jnp.where(
+        odd_sub,
+        jnp.where(even_lane, lane_roll(corner_se[...], -1), lane_roll(corner_sw[...], 1)),
+        jnp.where(even_lane, lane_roll(corner_ne[...], -1), lane_roll(corner_nw[...], 1)),
+    )
+    count = corners.shape[0]
+    for i in range(count):
+        corners[i] = lane_roll(dense, -(2 * i + 1))
+    for k in range(half):
+        places = turned(lane_roll(dense, -(2 * (count + k) + 1)))
+        for i in range(2):
+            j = 2 * k + i
+            south_face = places[i][1]
+            shares[j, 0] = jnp.where(bottom, jnp.minimum(south_face, 0.0), 0.0)
+            shares[j, 1] = jnp.where(
+                bottom,
+                jnp.maximum(south_face, 0.0),
+                jnp.where(top, jnp.maximum(-sides_y[j], 0.0), 0.0),
+            )
+
+
 def transport_and_solve(
     fields,
     levels,
@@ -306,11 +345,8 @@
     west,
     next_sides,
     west_x,
-    sides_y,
-    corner_sw,
-    corner_se,
-    corner_nw,
-    corner_ne,
+    corners,
+    shares,
     decay,
     source,
     state,
@@ -333,20 +369,6 @@
     top = local == rows - 1
     in_first = bottom | top
 
-    even_lane = lane % 2 == 0
-    dense = jnp.where(
-        odd_sub,
-        jnp.where(even_lane, lane_roll(corner_se[...], -1), lane_roll(corner_sw[...], 1)),
-        jnp.where(even_lane, lane_roll(corner_ne[...], -1), lane_roll(corner_nw[...], 1)),
-    )
-
-    def corner(slot, k):
-        return pltpu.roll(dense, lanes - 2 * (slot * half + k) - 1, 1)
-
-
-    def turned(value):
-        up, down = sub_roll(value, rows - 1), sub_roll(value, 1 - rows)
-        return ((up, down), (down, up))
 
     def inner_rows(first, second):
         (first_up, first_down), _ = turned(first)
@@ -369,7 +391,9 @@
         )
         north_x = jnp.where(in_first, sub_roll(packed_north, -t), sub_roll(packed_north, 5 - t))
         halo_x = jnp.where(odd_sub, south_x, north_x)
-        halo_west = jnp.where(first_lane, corner(fields, k), lane_roll(halo_x, 1))
+        halo_west = jnp.where(
+            first_lane, corners[fields * half + k], lane_roll(halo_x, 1)
+        )
         _, inner_top = inner_rows(cy[2 * k], cy[2 * k + 1])
         face = jnp.where(odd_sub, -south_y, inner_top)
         halo_coefs[k, 0] = (
@@ -382,19 +406,11 @@
         halo_coefs[k, 2] = jnp.maximum(halo_west, 0.0)
         halo_coefs[k, 3] = jnp.maximum(face, 0.0)
         places = turned(south_y)
-        edge_places = turned(corner(fields + 1, k))
         for i in range(2):
             j = 2 * k + i
             below = jnp.where(bottom, places[i][1], sub_roll(cy[j], 1))
             for c, value in enumerate(coefficients(cx[j], west_x[j], cy[j], below)):
                 own_coefs[j, c] = value
-            south_face = edge_places[i][1]
-            own_coefs[j, 5] = jnp.where(bottom, jnp.minimum(south_face, 0.0), 0.0)
-            own_coefs[j, 6] = jnp.where(
-                bottom,
-                jnp.maximum(south_face, 0.0),
-                jnp.where(top, jnp.maximum(-sides_y[j], 0.0), 0.0),
-            )
 
     def advect(f, k, own_set, halo_set):
         message_south = from_south[f * half + k]
@@ -403,7 +419,7 @@
         own = [tracers[slot] for slot in slots]
         own_east = [east[slot] for slot in slots]
         own_west = [west[slot] for slot in slots]
-        sides = corner(f, k)
+        sides = corners[f * half + k]
         halo = jnp.where(odd_sub, message_south, message_north)
         inner_bottom, inner_top = inner_rows(*own)
         flux = jnp.where(odd_sub, sub_roll(message_south, 1), sub_roll(message_north, -1))
@@ -451,7 +467,11 @@
         f2 = jnp.minimum(f1 + 1, fields - 1)
         columns = []
         for k in range(half):
-            own_set = [[own_coefs[2 * k + i, c] for c in range(7)] for i in range(2)]
+            own_set = [
+                [own_coefs[2 * k + i, c] for c in range(5)]
+                + [shares[2 * k + i, c] for c in range(2)]
+                for i in range(2)
+            ]
             halo_set = [halo_coefs[k, c] for c in range(4)]
             for one, two in zip(
                 advect(f1, k, own_set, halo_set), advect(f2, k, own_set, halo_set)
@@ -487,7 +507,7 @@
 
 
 def main_kernel(fields, levels, *refs):
-    inputs, (target, onehot), (state, placed), coefs = refs[:16], refs[16:18], refs[18:20], refs[20:]
+    inputs, (target, onehot), (state, placed), coefs = refs[:13], refs[13:15], refs[15:17], refs[17:]
     rows, lanes = target.shape
     total = transport_and_solve(fields, levels, *inputs, state, *coefs)
 
@@ -607,20 +627,27 @@
         out_specs=[VMEM] * 2,
         compiler_params=PARAMS,
     )(flat, edge, edge_west, edge_east)
-    edge_columns = pl.pallas_call(
+    next_sides, west_x, sides_y = pl.pallas_call(
         functools.partial(next_kernel, levels),
         out_shape=(array(fields * pairs, *tile),) + (array(pairs, *tile),) * 2,
         in_specs=[VMEM] * 4,
         out_specs=[VMEM] * 3,
         compiler_params=PARAMS,
     )(cx, edge, edge_west, edge_east)
+    corners, shares = pl.pallas_call(
+        functools.partial(corner_kernel, levels),
+        out_shape=(array((fields + 1) * half, *tile), array(pairs, 2, *tile)),
+        in_specs=[VMEM] * 5,
+        out_specs=[VMEM] * 2,
+        compiler_params=PARAMS,
+    )(sides_y, corner_sw, corner_se, corner_nw, corner_ne)
     state, placed = pl.pallas_call(
         functools.partial(main_kernel, fields, levels),
         out_shape=(array(fields * pairs, *tile), array(wide * rows, cols)),
-        in_specs=[VMEM] * 18,
+        in_specs=[VMEM] * 15,
         out_specs=[VMEM] * 2,
         scratch_shapes=[
-            pltpu.VMEM((pairs, 7) + tile, F32),
+            pltpu.VMEM((pairs, 5) + tile, F32),
             pltpu.VMEM((half, 4) + tile, F32),
         ],
         compiler_params=PARAMS,
@@ -631,11 +658,10 @@
         from_south,
         from_north,
         *shifted,
-        *edge_columns,
-        corner_sw,
-        corner_se,
-        corner_nw,
-        corner_ne,
+        next_sides,
+        west_x,
+        corners,
+        shares,
         decay,
         source,
         span_target,

time: 32 us -> 32 us (level)
  transfers between devices with their start and end apart: 5 -> 5, of which waited for: 2 -> 2; matrix products, arithmetic and copies ran while one was open for 0% -> 0% of each run, Pallas kernels for 11% -> 12%
where the time goes in v2:
time: 32 us; the launch traced here: 31.9 us
  blocking collectives  11.1 us (35%)
  starting transfers between devices  9.18 us (29%)
  Pallas kernels  7.03 us (22%)
  waiting for transfers between devices  3.83 us (12%)
  between operations  0.73 us (2%)
    all_to_all x1, blocking collectives, body(): lax.all_to_all(placed.reshape(wide, rows, cols), 'wide', split_axis=0, co...  11.1 us
    ppermute x5, starting transfers between devices, send(): return lax.ppermute(value, ('wide', 'narrow'), pairs_)  9.18 us
    ppermute x5, waiting for transfers between devices, send(): return lax.ppermute(value, ('wide', 'narrow'), pairs_)  3.83 us
    pallas_call x1, Pallas kernels, body(): pl.pallas_call(functools.partial(main_kernel, fields, levels), out_shape=...  1.44 us
    pallas_call x1, Pallas kernels, body(): pl.pallas_call(prep_kernel, out_shape=(array(levels, field_pairs, *tile),...  1.23 us
    pallas_call x1, Pallas kernels, body(): pl.pallas_call(functools.partial(shift_kernel, levels), out_shape=(array(...  1.22 us
    pallas_call x1, Pallas kernels, body(): pl.pallas_call(functools.partial(pack_north_kernel, levels), out_shape=(a...  1.13 us
    pallas_call x1, Pallas kernels, body(): pl.pallas_call(finish_kernel, out_shape=(array(rows, cols), array(fields...  0.78 us
  transfers between devices with their start and end apart: 5, of which 2 were waited for; matrix products, arithmetic and copies ran while one was open for 0% of the time, Pallas kernels for 12%

profile of v2, /device:TPU:0, one launch (start us, length us, event | category | flops | bytes accessed | tf_op | source)
XLA Modules:
  0.0 31.9 jit_solution(2006049906198844984)
XLA Ops:
  0.6 1.1 %shard_map.86 = (f32[104,8,128]{2,1,0:T(8,128)S(1)}, f32[8,8,128]{2,1,0:T(8,128)S(1)}, f32[8,8,128]{2,1,0:T(8,128)S(1)}, f32[56,8,128]{2,1,0:T(8,128)S(1)}) custom-call(f32[104,8,128]{2,1,0:T(8,128)} %bitcast.6, f32[8,8,128]{2,1,0:T(8,128)} %bitcast.7, f32[8,8,128]{2,1,0:T(8,128)} %bitcast.8), custom_call_target="tpu_custom_call" | custom-call | tf_op jit(solution)/shard_map/pallas_call | solution.py:569
  1.8 3.0 %collective-permute-start = (f32[56,8,128]{2,1,0:T(8,128)S(1)}, f32[56,8,128]{2,1,0:T(8,128)S(1)}, u32[]{:S(2)}, u32[]{:S(2)}) collective-permute-start(f32[56,8,128]{2,1,0:T(8,128)S(1)} %get-tuple-element.26), channel_id=1, source_target_pairs={{0,2},{1,3},{2,4},{3,5},{4,6},{5,7},{6,8},{7,9},{8,10},{9,11},{10,... | collective-permute-start | bytes 688136 | tf_op jit(solution)/shard_map/ppermute | solution.py:600
  4.8 0.6 %shard_map.87 = (f32[15,8,128]{2,1,0:T(8,128)S(1)}, f32[8,128]{1,0:T(8,128)S(1)}, f32[54,8,128]{2,1,0:T(8,128)S(1)}) custom-call(f32[104,8,128]{2,1,0:T(8,128)S(1)} %get-tuple-element.23.tracers.refs_0_, f32[8,8,128]{2,1,0:T(8,128)S(1)} %get-tuple-element.24.cx.refs_1_, f32[8,8,128]{2,1,0:T(8,128)S(1)} %get-tuple-element.25.cy.refs_2_), custom_call_target="tpu_custom_call" | custom-call | tf_op jit(solution)/shard_map/pallas_call | solution.py:582
  5.4 0.0 copy-start.1
  5.4 4.1 %collective-permute-start.1 = (f32[54,8,128]{2,1,0:T(8,128)S(1)}, f32[54,8,128]{2,1,0:T(8,128)S(1)}, u32[]{:S(2)}, u32[]{:S(2)}) collective-permute-start(f32[54,8,128]{2,1,0:T(8,128)S(1)} %get-tuple-element.27), channel_id=1, source_target_pairs={{0,30},{1,31},{2,0},{3,1},{4,2},{5,3},{6,4},{7,5},{8,6},{9,7},{10,... | collective-permute-start | bytes 663560 | tf_op jit(solution)/shard_map/ppermute | solution.py:600
  9.5 0.0 collective-permute-start.2
  9.5 2.1 %collective-permute-start.4 = (f32[8,128]{1,0:T(8,128)S(1)}, f32[8,128]{1,0:T(8,128)S(1)}, u32[]{:S(2)}, u32[]{:S(2)}) collective-permute-start(f32[8,128]{1,0:T(8,128)S(1)} %get-tuple-element.34), channel_id=1, source_target_pairs={{0,31},{1,30},{2,1},{3,0},{4,3},{5,2},{6,5},{7,4},{8,7},{9,6},{10,... | collective-permute-start | bytes 12296 | tf_op jit(solution)/shard_map/ppermute | solution.py:600
  11.6 0.0 collective-permute-start.3
  11.6 0.0 copy-done.3
  11.6 0.0 copy-done.1
  11.6 0.0 copy-done
  11.6 0.0 copy-done.2
  11.6 1.2 %shard_map.91 = (f32[16,7,8,128]{3,2,1,0:T(8,128)S(1)}, f32[16,7,8,128]{3,2,1,0:T(8,128)S(1)}, bf16[512,128]{1,0:T(8,128)(2,1)S(1)}) custom-call(f32[2,3,13]{2,1,0:T(4,128)S(1)} %copy.9.coeffs, f32[13,16]{1,0:T(8,128)S(1)} %copy-done.1, s32[4,128]{1,0:T(4,128)S(1)} %copy-done.2, s32[4,128]{1,0:T(4,128)S(1)} %copy-done), custom_call_target="tpu_custom_call" | custom-call | flops 4000000 | bytes 2000000 | tf_op jit(solution)/shard_map/pallas_call | solution.py:613
  12.9 0.0 collective-permute-done.2.edge_west.edge_east
  12.9 0.4 %shard_map.89 = (f32[104,8,128]{2,1,0:T(8,128)S(1)}, f32[8,8,128]{2,1,0:T(8,128)S(1)}, f32[8,8,128]{2,1,0:T(8,128)S(1)}) custom-call(f32[8,8,128]{2,1,0:T(8,128)S(1)} %get-tuple-element.24.cx.refs_1_, f32[15,8,128]{2,1,0:T(8,128)S(1)} %get-tuple-element.28.edge, f32[15,8,128]{2,1,0:T(8,128)S(1)} %collective-permute-done.2.edge_west.edge_east, ...), custom_call_target="tpu_custom_call" | custom-call | tf_op jit(solution)/shard_map/pallas_call | solution.py:630
  13.3 1.2 %shard_map.88 = (f32[104,8,128]{2,1,0:T(8,128)S(1)}, f32[104,8,128]{2,1,0:T(8,128)S(1)}) custom-call(f32[104,8,128]{2,1,0:T(8,128)S(1)} %get-tuple-element.23.tracers.refs_0_, f32[15,8,128]{2,1,0:T(8,128)S(1)} %get-tuple-element.28.edge, f32[15,8,128]{2,1,0:T(8,128)S(1)} %collective-permute-done.2.edge_west.edge_east, ...), custom_call_target="tpu_custom_call" | custom-call | tf_op jit(solution)/shard_map/pallas_call | solution.py:623
  14.5 0.7 %collective-permute-done.4.corner_nw.corner_ne = f32[8,128]{1,0:T(8,128)S(1)} collective-permute-done((f32[8,128]{1,0:T(8,128)S(1)}, f32[8,128]{1,0:T(8,128)S(1)}, u32[]{:S(2)}, u32[]{:S(2)}) %collective-permute-start.4) | collective-permute-done | bytes 4128 | tf_op jit(solution)/shard_map/ppermute | solution.py:600
  15.2 3.1 %collective-permute-done.3.corner_sw.corner_se = f32[8,128]{1,0:T(8,128)S(1)} collective-permute-done((f32[8,128]{1,0:T(8,128)S(1)}, f32[8,128]{1,0:T(8,128)S(1)}, u32[]{:S(2)}, u32[]{:S(2)}) %collective-permute-start.3) | collective-permute-done | bytes 4128 | tf_op jit(solution)/shard_map/ppermute | solution.py:600
  18.3 0.2 shard_map.90
  18.5 0.0 collective-permute-done.1.refs_4_
  18.5 0.0 collective-permute-done.refs_3_
  18.6 1.4 %shard_map.92 = (f32[104,8,128]{2,1,0:T(8,128)S(1)}, f32[64,128]{1,0:T(8,128)S(1)}) custom-call(f32[104,8,128]{2,1,0:T(8,128)S(1)} %get-tuple-element.23.tracers.refs_0_, f32[8,8,128]{2,1,0:T(8,128)S(1)} %get-tuple-element.24.cx.refs_1_, f32[8,8,128]{2,1,0:T(8,128)S(1)} %get-tuple-element.25.cy.refs_2_, f32[56,8,128]{2,1,0:T(8,128)S(1)} %collective-permute-done.refs_3_, ...), custom_call_target="tpu_custom_call" | custom-call | tf_op jit(solution)/shard_map/pallas_call | solution.py:644
  20.0 11.1 %all_to_all.5.parts = f32[16,4,128]{2,1,0:T(4,128)S(1)} all-to-all(f32[16,4,128]{2,1,0:T(4,128)S(1)} %bitcast.5), channel_id=1, replica_groups=mesh['wide'=16,'narrow'=2] {'wide'}, dimensions={0} | all-to-all | bytes 65536 | tf_op jit(solution)/shard_map/all_to_all | solution.py:670
  31.1 0.8 %shard_map.93 = (f32[4,128]{1,0:T(4,128)}, f32[104,8,128]{2,1,0:T(8,128)}) custom-call(f32[16,4,128]{2,1,0:T(4,128)S(1)} %all_to_all.5.parts, f32[104,8,128]{2,1,0:T(8,128)S(1)} %get-tuple-element.41.state), custom_call_target="tpu_custom_call" | custom-call | tf_op jit(solution)/shard_map/pallas_call | solution.py:673
  (4 shorter events, 0.0 us)
Async XLA Ops:
  1.8 16.8 %collective-permute-start = (f32[56,8,128]{2,1,0:T(8,128)S(1)}, f32[56,8,128]{2,1,0:T(8,128)S(1)}, u32[]{:S(2)}, u32[]{:S(2)}) collective-permute-start(f32[56,8,128]{2,1,0:T(8,128)S(1)} %get-tuple-element.26), channel_id=1, source_target_pairs={{0,2},{1,3},{2,4},{3,5},{4,6},{5,7},{6,8},{7,9},{8,10},{9,11},{10,... | collective-permute-start | bytes 688136 | tf_op jit(solution)/shard_map/ppermute | solution.py:600
  4.8 6.8 %copy-start.3 = (f32[2,3,13]{2,0,1:T(2,128)S(1)}, f32[2,3,13]{2,0,1:T(2,128)}, u32[]{:S(2)}) copy-start(f32[2,3,13]{2,0,1:T(2,128)} %param.11) | copy-start | bytes 940
  5.4 6.2 %copy-start.1 = (f32[13,16]{1,0:T(8,128)S(1)}, f32[13,16]{1,0:T(8,128)}, u32[]{:S(2)}) copy-start(f32[13,16]{1,0:T(8,128)} %profile.1) | copy-start | bytes 2500
  5.4 13.1 %collective-permute-start.1 = (f32[54,8,128]{2,1,0:T(8,128)S(1)}, f32[54,8,128]{2,1,0:T(8,128)S(1)}, u32[]{:S(2)}, u32[]{:S(2)}) collective-permute-start(f32[54,8,128]{2,1,0:T(8,128)S(1)} %get-tuple-element.27), channel_id=1, source_target_pairs={{0,30},{1,31},{2,0},{3,1},{4,2},{5,3},{6,4},{7,5},{8,6},{9,7},{10,... | collective-permute-start | bytes 663560 | tf_op jit(solution)/shard_map/ppermute | solution.py:600
  9.5 3.4 %collective-permute-start.2 = (f32[15,8,128]{2,1,0:T(8,128)S(1)}, f32[15,8,128]{2,1,0:T(8,128)S(1)}, u32[]{:S(2)}, u32[]{:S(2)}) collective-permute-start(f32[15,8,128]{2,1,0:T(8,128)S(1)} %get-tuple-element.28.edge), channel_id=1, source_target_pairs={{0,1},{1,0},{2,3},{3,2},{4,5},{5,4},{6,7},{7,6},{8,9},{9,8},{10,11... | collective-permute-start | bytes 184328 | tf_op jit(solution)/shard_map/ppermute | solution.py:600
  9.5 2.1 %copy-start = (s32[4,128]{1,0:T(4,128)S(1)}, s32[4,128]{1,0:T(4,128)}, u32[]{:S(2)}) copy-start(s32[4,128]{1,0:T(4,128)} %refs_13_.1) | copy-start | bytes 6148
  9.5 2.1 %copy-start.2 = (s32[4,128]{1,0:T(4,128)S(1)}, s32[4,128]{1,0:T(4,128)}, u32[]{:S(2)}) copy-start(s32[4,128]{1,0:T(4,128)} %klass.1) | copy-start | bytes 6148
  9.5 5.8 %collective-permute-start.4 = (f32[8,128]{1,0:T(8,128)S(1)}, f32[8,128]{1,0:T(8,128)S(1)}, u32[]{:S(2)}, u32[]{:S(2)}) collective-permute-start(f32[8,128]{1,0:T(8,128)S(1)} %get-tuple-element.34), channel_id=1, source_target_pairs={{0,31},{1,30},{2,1},{3,0},{4,3},{5,2},{6,5},{7,4},{8,7},{9,6},{10,... | collective-permute-start | bytes 12296 | tf_op jit(solution)/shard_map/ppermute | solution.py:600
  11.6 6.7 %collective-permute-start.3 = (f32[8,128]{1,0:T(8,128)S(1)}, f32[8,128]{1,0:T(8,128)S(1)}, u32[]{:S(2)}, u32[]{:S(2)}) collective-permute-start(f32[8,128]{1,0:T(8,128)S(1)} %get-tuple-element.34), channel_id=1, source_target_pairs={{0,3},{1,2},{2,5},{3,4},{4,7},{5,6},{6,9},{7,8},{8,11},{9,10},{10,... | collective-permute-start | bytes 12296 | tf_op jit(solution)/shard_map/ppermute | solution.py:600
